TPU v7x, 512 devices: a whole 4x4x16 slice. The times are simulated.
512 devices in a mesh: row: 32 (over y, x, core), col: 16 (over z).
Axes of the slice: x: 4, y: 4, z: 16, core: 2. Of those that a mesh axis runs over, the one named last changes fastest.
Arguments:
- iterate_t: bfloat16 [32, 16, 64, 32768], P(None, 'col', None, 'row'), may hold values from -0.03125 to 0.03125
- vectors: bfloat16 [32768, 256], P(('row', 'col')), may hold values from -6 to 6
- old_factor_t: bfloat16 [512, 32768], P('col', 'row'), may hold values from -5 to 5
Outputs:
- panel: float32 [32768, 256], P(('row', 'col'))
- basis: float32 [768, 32768], P('col', 'row')
All inputs are finite; a program needn't handle non-finite values.
Results may differ from a plain program's by a relative error of at most 0.0013.
Values may be sent and summed in bfloat16 or wider, within the bound.
A program may use at most 64 MiB of HBM per device.

v0:
```python
import jax
import jax.numpy as jnp
from jax import lax
from jax.sharding import PartitionSpec as P

NSTATE = 32768


def body(iterate_t, vectors, old_factor_t):
    flat_iterate = iterate_t.reshape(-1, iterate_t.shape[-1])
    highest = lax.Precision.HIGHEST

    def apply_iterate(vector):
        gathered = lax.all_gather(vector, "row", axis=0, tiled=True)
        return lax.psum_scatter(
            lax.dot_general(
                flat_iterate, gathered, (((0,), (0,)), ((), ())), preferred_element_type=jnp.float32
            ),
            "col",
            scatter_dimension=0,
            tiled=True,
        )

    first_full = apply_iterate(vectors)
    second = apply_iterate(first_full.astype(jnp.bfloat16)).astype(jnp.bfloat16)
    panel = 1.5 * first_full - 0.5 * apply_iterate(second)
    old_gathered = lax.all_gather(old_factor_t, "col", axis=0, tiled=True)
    panel_gathered = lax.all_gather(panel, "col", axis=0, tiled=True)
    old_full = old_gathered.astype(jnp.float32)
    scale_gram = 1.0 / NSTATE
    column = lax.axis_index("col")
    groups = lax.axis_size("col")
    panel_share = panel.shape[1] // groups
    own_panel = lax.dynamic_slice_in_dim(panel_gathered, column * panel_share, panel_share, 1)
    own_old = old_factor_t.astype(jnp.float32)
    old_columns = (
        jnp.concatenate(
            [
                lax.dot_general(
                    old_gathered,
                    old_factor_t,
                    (((1,), (1,)), ((), ())),
                    preferred_element_type=jnp.float32,
                ),
                lax.dot_general(
                    panel_gathered, own_old, (((0,), (1,)), ((), ())), precision=highest
                ),
            ],
            0,
        )
        * scale_gram
    )
    panel_columns = (
        jnp.concatenate(
            [
                jnp.dot(old_full, own_panel, precision=highest),
                lax.dot_general(
                    panel_gathered, own_panel, (((0,), (0,)), ((), ())), precision=highest
                ),
            ],
            0,
        )
        * scale_gram
    )
    summed_old, summed_panel = lax.psum((old_columns, panel_columns), "row")
    left_part, right_part = (
        lax.all_gather(summed_old, "col", axis=1, tiled=True),
        lax.all_gather(summed_panel, "col", axis=1, tiled=True),
    )
    gram = jnp.concatenate([left_part, right_part], 1)
    lower_factor = jnp.linalg.cholesky(gram)
    identity = jnp.eye(gram.shape[0], dtype=jnp.float32)
    inverse = jax.scipy.linalg.solve_triangular(lower_factor, identity, lower=True)
    basis_share = gram.shape[0] // groups
    inverse_rows = lax.dynamic_slice_in_dim(inverse, column * basis_share, basis_share, 0)
    old_count = old_gathered.shape[0]
    basis = jnp.dot(inverse_rows[:, :old_count], old_full, precision=highest)
    basis = basis + lax.dot_general(
        inverse_rows[:, old_count:], panel_gathered, (((1,), (1,)), ((), ())), precision=highest
    )
    return (panel, basis)


def solution(mesh):
    return jax.shard_map(
        body,
        mesh=mesh,
        in_specs=(P(None, "col", None, "row"), P(("row", "col"), None), P("col", "row")),
        out_specs=(P(("row", "col"), None), P("col", "row")),
        check_vma=False,
    )
```

profile of v0, /device:TPU:32, one launch (start us, length us, event | category | flops | bytes accessed | tf_op | source)
XLA Modules:
  0.0 1116.8 jit_solution(5605788853649218226)
XLA Ops:
  7.9 65.4 %all-gather.7.cloned.1.call-done = bf16[2048,256]{1,0:T(8,128)(2,1)} async-done(((bf16[64,256]{1,0:T(8,128)(2,1)}), bf16[2048,256]{1,0:T(8,128)(2,1)}) %all-gather.7.cloned.1.call-update) | async-done | bytes 1048592 | tf_op jit(solution)/shard_map/all_gather | solution.py:14
  73.4 4.7 fusion.64
  78.2 69.4 %reduce-scatter.6.cloned.1.call-done = f32[64,256]{1,0:T(8,128)} async-done(((f32[1024,256]{1,0:T(8,128)}), f32[64,256]{1,0:T(8,128)}) %reduce-scatter.6.cloned.1.call-update) | async-done | bytes 65552 | tf_op jit(solution)/shard_map/reduce_scatter | solution.py:15
  147.5 1.5 convert_element_type.19
  149.1 59.0 %all-gather.9.cloned.1.call-done = bf16[2048,256]{1,0:T(8,128)(2,1)} async-done(((bf16[64,256]{1,0:T(8,128)(2,1)}), bf16[2048,256]{1,0:T(8,128)(2,1)}) %all-gather.9.cloned.1.call-update) | async-done | bytes 1048592 | tf_op jit(solution)/shard_map/all_gather | solution.py:14
  208.1 3.8 convolution_bitcast_fusion.1
  211.9 1.3 copy.14
  213.3 69.4 %reduce-scatter.10.cloned.1.call-done = f32[64,256]{1,0:T(8,128)} async-done(((f32[1024,256]{1,0:T(8,128)}), f32[64,256]{1,0:T(8,128)}) %reduce-scatter.10.cloned.1.call-update) | async-done | bytes 65552 | tf_op jit(solution)/shard_map/reduce_scatter | solution.py:15
  282.7 1.5 convert_element_type.20
  284.2 58.4 %all-gather.11.cloned.1.call-done = bf16[2048,256]{1,0:T(8,128)(2,1)} async-done(((bf16[64,256]{1,0:T(8,128)(2,1)}), bf16[2048,256]{1,0:T(8,128)(2,1)}) %all-gather.11.cloned.1.call-update) | async-done | bytes 1048592 | tf_op jit(solution)/shard_map/all_gather | solution.py:14
  342.6 5.3 convolution_bitcast_fusion
  348.7 68.6 %reduce-scatter.8.cloned.1.call-done = f32[64,256]{1,0:T(8,128)} async-done(((f32[1024,256]{1,0:T(8,128)}), f32[64,256]{1,0:T(8,128)}) %reduce-scatter.8.cloned.1.call-update) | async-done | bytes 65552 | tf_op jit(solution)/shard_map/reduce_scatter | solution.py:15
  417.3 1.5 multiply_subtract_fusion
  418.9 70.0 %all-gather.13.cloned.1.call-done = bf16[512,1024]{1,0:T(8,128)(2,1)} async-done(((bf16[32,1024]{1,0:T(8,128)(2,1)}), bf16[512,1024]{1,0:T(8,128)(2,1)}) %all-gather.13.cloned.1.call-update) | async-done | bytes 1048592 | tf_op jit(solution)/shard_map/all_gather | solution.py:27
  488.9 1.6 fusion.65
  490.5 69.3 %all-gather.15.cloned.1.call-done = f32[1024,256]{1,0:T(8,128)} async-done(((f32[64,256]{1,0:T(8,128)}), f32[1024,256]{1,0:T(8,128)}) %all-gather.15.cloned.1.call-update) | async-done | bytes 1048592 | tf_op jit(solution)/shard_map/all_gather | solution.py:28
  559.8 1.8 fusion.66
  562.3 127.3 %all-reduce.3.cloned.1.call-done = f32[768,32]{0,1:T(8,128)} async-done(((f32[768,32]{0,1:T(8,128)}), f32[768,32]{0,1:T(8,128)}) %all-reduce.3.cloned.1.call-update) | async-done | bytes 98320 | tf_op jit(solution)/shard_map/psum | solution.py:65
  690.6 1.6 fusion.20
  692.2 1.1 fusion.24
  693.3 1.2 convolution_bitcast_fusion.2
  694.5 125.5 %psum.15 = f32[768,16]{0,1:T(8,128)S(1)} all-reduce(f32[768,16]{0,1:T(8,128)S(1)} %maximum_multiply_fusion.1), channel_id=1, replica_groups=mesh['row'=32,'col'=16] {'row'}, use_global_device_ids=true, to_apply=%region_4.0 | all-reduce | flops 12288 | bytes 98304 | tf_op jit(solution)/shard_map/psum | solution.py:65
  820.0 36.1 %all_gather.27 = f32[768,256]{0,1:T(8,128)} all-gather(f32[768,16]{0,1:T(8,128)S(1)} %psum.15), channel_id=1, replica_groups=mesh['row'=32,'col'=16] {'col'}, dimensions={1}, use_global_device_ids=true | all-gather | bytes 835584 | tf_op jit(solution)/shard_map/all_gather | solution.py:68
  856.1 1.6 constant_dynamic-update-slice_fusion.1
  857.8 2.1 copy.12
  860.0 2.0 fusion
  861.9 1.4 copy-done.4
  863.4 11.7 %cholesky.165 = f32[128,128]{1,0:T(8,128)S(1)} custom-call(f32[128,128]{1,0:T(8,128)S(1)} %cholesky.424), custom_call_target="Cholesky" | custom-call | tf_op jit(solution)/shard_map/jit(cholesky)/cholesky | solution.py:71
  875.1 9.8 custom-call.47
  885.1 1.4 constant_dynamic-update-slice_fusion.16
  886.5 1.4 convolution_subtract_fusion.4
  888.6 11.7 %cholesky.188 = f32[128,128]{1,0:T(8,128)S(1)} custom-call(f32[128,128]{1,0:T(8,128)S(1)} %cholesky.428), custom_call_target="Cholesky" | custom-call | tf_op jit(solution)/shard_map/jit(cholesky)/cholesky | solution.py:71
  900.4 10.0 custom-call.48
  910.4 1.3 convolution_dynamic-update-slice_fusion.1
  911.7 1.5 convolution_subtract_fusion.5
  913.9 11.7 %cholesky.354 = f32[128,128]{1,0:T(8,128)S(1)} custom-call(f32[128,128]{1,0:T(8,128)S(1)} %cholesky.433), custom_call_target="Cholesky" | custom-call | tf_op jit(solution)/shard_map/jit(cholesky)/cholesky | solution.py:71
  926.3 9.8 custom-call.49
  936.1 1.2 convolution_dynamic-update-slice_fusion.2
  937.4 1.6 convolution_subtract_fusion.6
  939.6 12.1 %cholesky.373 = f32[128,128]{1,0:T(8,128)S(1)} custom-call(f32[128,128]{1,0:T(8,128)S(1)} %cholesky.438), custom_call_target="Cholesky" | custom-call | tf_op jit(solution)/shard_map/jit(cholesky)/cholesky | solution.py:71
  952.5 9.8 custom-call.50
  962.3 1.2 convolution_dynamic-update-slice_fusion.3
  963.4 1.5 convolution_subtract_fusion.7
  965.6 13.2 %cholesky.392 = f32[128,128]{1,0:T(8,128)} custom-call(f32[128,128]{1,0:T(8,128)} %cholesky.443), custom_call_target="Cholesky" | custom-call | tf_op jit(solution)/shard_map/jit(cholesky)/cholesky | solution.py:71
  978.8 1.5 select_reduce_fusion.1
  980.9 11.3 %custom-call.51 = f32[1,128,128]{1,2,0:T(8,128)} custom-call(f32[1,128,128]{2,1,0:T(8,128)} %get-tuple-element.33), custom_call_target="InvertDiagBlocksLowerTriangular" | custom-call | tf_op jit(solution)/shard_map/jit(cholesky)/cholesky | solution.py:71
  993.3 1.3 convolution_subtract_fusion.8
  994.6 11.9 %cholesky.410 = f32[128,128]{1,0:T(8,128)S(1)} custom-call(f32[128,128]{1,0:T(8,128)S(1)} %convolution_subtract_fusion.8), custom_call_target="Cholesky" | custom-call | tf_op jit(solution)/shard_map/jit(cholesky)/cholesky | solution.py:71
  1011.6 1.6 select_select_fusion
  1013.2 20.6 %while.1 = (s32[]{:T(128)}, f32[768,768]{1,0:T(8,128)}, s32[6,2]{0,1:T(2,128)S(1)}, f32[6,128,128]{2,1,0:T(8,128)}, s32[]{:T(128)}) while((s32[]{:T(128)}, f32[768,768]{1,0:T(8,128)}, s32[6,2]{0,1:T(2,128)S(1)}, f32[6,128,128]{2,1,0:T(8,128)}, s32[]{:T(128)}) %tuple.44), condition=%wide.while_cond, body=%wide.while_body.sunk | while | flops 2 | bytes 132705 | solution.py:73
  1013.8 2.9 bitcast_dynamic-update-slice_fusion.2
  1017.4 2.8 bitcast_dynamic-update-slice_fusion.2
  1020.8 2.8 bitcast_dynamic-update-slice_fusion.2
  1024.2 2.8 bitcast_dynamic-update-slice_fusion.2
  1027.7 2.8 bitcast_dynamic-update-slice_fusion.2
  1031.1 2.8 bitcast_dynamic-update-slice_fusion.2
  1033.9 60.4 %custom-call.52 = f32[6,128,128]{1,2,0:T(8,128)} custom-call(f32[6,128,128]{2,1,0:T(8,128)} %get-tuple-element.9), custom_call_target="InvertDiagBlocksLowerTriangular" | custom-call | tf_op jit(solution)/shard_map/jit(_solve_triangular)/triangular_solve | solution.py:73
  1094.2 1.3 constant_dynamic-update-slice_fusion.6
  1095.5 1.5 convolution_subtract_fusion.2
  1097.6 1.5 convolution_subtract_fusion.3
  1099.6 1.8 convolution_subtract_fusion.1
  1102.0 2.0 fusion.9
  1104.5 2.3 convolution_subtract_fusion
  1108.0 1.8 convolution_add_fusion
  (86 shorter events, 18.0 us)
Async XLA Ops:
  7.2 66.2 %all-gather.7.cloned.1.call-start = ((), (), s32[]{:S(2)}) async-start(), calls=%async_computation.3 | async-start | bytes 1081344 | tf_op jit(solution)/shard_map/all_gather | solution.py:14
  7.9 139.6 %reduce-scatter.6.cloned.1.call-start = ((), (), s32[]{:S(2)}) async-start(), calls=%async_computation.4 | async-start | bytes 1114112 | tf_op jit(solution)/shard_map/reduce_scatter | solution.py:15
  78.1 130.0 %all-gather.9.cloned.1.call-start = ((), (), s32[]{:S(2)}) async-start(), calls=%async_computation.5 | async-start | bytes 1081344 | tf_op jit(solution)/shard_map/all_gather | solution.py:14
  149.0 133.7 %reduce-scatter.10.cloned.1.call-start = ((), (), s32[]{:S(2)}) async-start(), calls=%async_computation.12 | async-start | bytes 1114112 | tf_op jit(solution)/shard_map/reduce_scatter | solution.py:15
  213.2 129.4 %all-gather.11.cloned.1.call-start = ((), (), s32[]{:S(2)}) async-start(), calls=%async_computation.6 | async-start | bytes 1081344 | tf_op jit(solution)/shard_map/all_gather | solution.py:14
  284.2 133.2 %copy-start.11 = (f32[64,256]{1,0:T(8,128)S(1)}, f32[64,256]{1,0:T(8,128)}, u32[]{:S(2)}) copy-start(f32[64,256]{1,0:T(8,128)} %reduce-scatter.6.cloned.1.call-done) | copy-start | bytes 196612
  284.2 204.7 %copy-start.9 = (bf16[32,1024]{1,0:T(8,128)(2,1)S(1)}, bf16[32,1024]{1,0:T(8,128)(2,1)}, u32[]{:S(2)}) copy-start(bf16[32,1024]{1,0:T(8,128)(2,1)} %param.5) | copy-start | bytes 196612
  284.2 133.1 %reduce-scatter.8.cloned.1.call-start = ((), (), s32[]{:S(2)}) async-start(), calls=%async_computation.7 | async-start | bytes 1114112 | tf_op jit(solution)/shard_map/reduce_scatter | solution.py:15
  347.9 141.0 %all-gather.13.cloned.1.call-start = ((), (), s32[]{:S(2)}) async-start(), calls=%async_computation.8 | async-start | bytes 1114112 | tf_op jit(solution)/shard_map/all_gather | solution.py:27
  348.7 211.1 %all-gather.15.cloned.1.call-start = ((), (), s32[]{:S(2)}) async-start(), calls=%async_computation.9 | async-start | bytes 1114112 | tf_op jit(solution)/shard_map/all_gather | solution.py:28
  418.8 270.7 %all-reduce.3.cloned.1.call-start = ((), (), s32[]{:S(2)}) async-start(), calls=%async_computation.10 | async-start | bytes 196608 | tf_op jit(solution)/shard_map/psum | solution.py:65
  559.8 132.4 %copy-start = (f32[1024,256]{1,0:T(8,128)S(1)}, f32[1024,256]{1,0:T(8,128)}, u32[]{:S(2)}) copy-start(f32[1024,256]{1,0:T(8,128)} %all-gather.15.cloned.1.call-done) | copy-start | bytes 3145732
  561.6 131.8 %copy-start.1 = (bf16[512,1024]{1,0:T(8,128)(2,1)S(1)}, bf16[512,1024]{1,0:T(8,128)(2,1)}, u32[]{:S(2)}) copy-start(bf16[512,1024]{1,0:T(8,128)(2,1)} %all-gather.13.cloned.1.call-done) | copy-start | bytes 3145732
  562.3 293.9 %all-gather.17.cloned.1.call-start = ((), (), s32[]{:S(2)}) async-start(), calls=%async_computation.11 | async-start | bytes 1671168 | tf_op jit(solution)/shard_map/all_gather | solution.py:67
  856.1 1.6 copy-start.5
  861.9 1.5 copy-start.4
  887.9 0.7 copy-start.6
  913.2 0.7 copy-start.7
  938.9 0.7 copy-start.8
  1013.2 84.4 %copy-start.3 = (f32[768,768]{1,0:T(8,128)S(1)}, f32[768,768]{1,0:T(8,128)}, u32[]{:S(2)}) copy-start(f32[768,768]{1,0:T(8,128)} %fusion.20) | copy-start | bytes 7077892
  1094.2 2.8 copy-start.10
  1104.0 3.4 copy-start.2
Sparse Core Ops, SparseCore 0:
  11.1 62.1 all-gather.6
  78.2 69.2 reduce-scatter.5
  151.7 56.3 all-gather.8
  213.4 69.2 reduce-scatter.9
  286.2 56.3 all-gather.10
  348.0 69.2 reduce-scatter.7
  419.6 69.2 all-gather.12
  491.7 67.9 all-gather.14
  564.0 125.5 all-reduce.2
  691.5 71.4 all-gather.16
where the time goes:
time: 1120 us
  waiting for transfers between devices  658 us (59%)
  other arithmetic  200 us (18%)
  blocking collectives  162 us (14%)
  matrix products  48.3 us (4%)
  local copies, waits for them, and re-layouts  30.1 us (3%)
  between operations  18.5 us (2%)
    reduce_scatter x3, waiting for transfers between devices, apply_iterate(): lax.psum_scatter(lax.dot_general(flat_iterate, gathered, (((0,), (0,)), (...  207 us
    all_gather x3, waiting for transfers between devices, apply_iterate(): gathered = lax.all_gather(vector, 'row', axis=0, tiled=True)  183 us
    another operation x22, other arithmetic, body(): lower_factor = jnp.linalg.cholesky(gram)  128 us
    psum x1, waiting for transfers between devices, body(): summed_old, summed_panel = lax.psum((old_columns, panel_columns), 'row')  127 us
    psum x1, blocking collectives, body(): summed_old, summed_panel = lax.psum((old_columns, panel_columns), 'row')  125 us
    all_gather x1, waiting for transfers between devices, body(): old_gathered = lax.all_gather(old_factor_t, 'col', axis=0, tiled=True)  70 us
    all_gather x1, waiting for transfers between devices, body(): panel_gathered = lax.all_gather(panel, 'col', axis=0, tiled=True)  69.3 us
    another operation x3, other arithmetic, body(): jax.scipy.linalg.solve_triangular(lower_factor, identity, lower=True)  62 us
  transfers between devices with their start and end apart: 10, of which 9 were waited for; matrix products, arithmetic and copies ran while one was open for 1% of the time, Pallas kernels for 0%

commit v1 on v0

--- a/solution.py
+++ b/solution.py
@@ -6,12 +6,19 @@
 NSTATE = 32768
 
 
+def swapped_in(value, name, d):
+    count = lax.axis_size(name)
+    blocks = jnp.stack([value for _ in range(count)])
+    blocks = lax.all_to_all(blocks, name, split_axis=0, concat_axis=0)
+    return jnp.concatenate(blocks, axis=d)
+
+
 def body(iterate_t, vectors, old_factor_t):
     flat_iterate = iterate_t.reshape(-1, iterate_t.shape[-1])
     highest = lax.Precision.HIGHEST
 
     def apply_iterate(vector):
-        gathered = lax.all_gather(vector, "row", axis=0, tiled=True)
+        gathered = swapped_in(vector, "row", 0)
         return lax.psum_scatter(
             lax.dot_general(
                 flat_iterate, gathered, (((0,), (0,)), ((), ())), preferred_element_type=jnp.float32

time: 1120 us -> 1010 us (0.902)
  waiting for transfers between devices: 658 us -> 466 us
  blocking collectives: 162 us -> 235 us
    all_gather x3 -> x0, waiting for transfers between devices: 183 us -> none  [apply_iterate(): gathered = lax.all_gather(vector, 'row', axis=0, tiled=True)]
    all_to_all x0 -> x3, blocking collectives: none -> 72.9 us  [swapped_in(): blocks = lax.all_to_all(blocks, name, split_axis=0, concat_axis=0)]
    another operation x18 -> x21, local copies, waits for them, and re-layouts: 20.6 us -> 22.6 us
  transfers between devices with their start and end apart: 10 -> 7, of which waited for: 9 -> 6; matrix products, arithmetic and copies ran while one was open for 1% -> 1% of each run, Pallas kernels for 0% -> 0%
where the time goes in v1:
time: 1010 us; the launch traced here: 997 us
  waiting for transfers between devices  466 us (46%)
  blocking collectives  235 us (23%)
  other arithmetic  198 us (20%)
  matrix products  47.5 us (5%)
  local copies, waits for them, and re-layouts  32.1 us (3%)
  between operations  18.6 us (2%)
    reduce_scatter x3, waiting for transfers between devices, apply_iterate(): lax.psum_scatter(lax.dot_general(flat_iterate, gathered, (((0,), (0,)), (...  199 us
    another operation x22, other arithmetic, body(): lower_factor = jnp.linalg.cholesky(gram)  128 us
    psum x1, waiting for transfers between devices, body(): summed_old, summed_panel = lax.psum((old_columns, panel_columns), 'row')  127 us
    psum x1, blocking collectives, body(): summed_old, summed_panel = lax.psum((old_columns, panel_columns), 'row')  125 us
    all_to_all x3, blocking collectives, swapped_in(): blocks = lax.all_to_all(blocks, name, split_axis=0, concat_axis=0)  72.9 us
    all_gather x1, waiting for transfers between devices, body(): old_gathered = lax.all_gather(old_factor_t, 'col', axis=0, tiled=True)  69.8 us
    all_gather x1, waiting for transfers between devices, body(): panel_gathered = lax.all_gather(panel, 'col', axis=0, tiled=True)  69 us
    another operation x3, other arithmetic, body(): jax.scipy.linalg.solve_triangular(lower_factor, identity, lower=True)  62 us
  transfers between devices with their start and end apart: 7, of which 6 were waited for; matrix products, arithmetic and copies ran while one was open for 1% of the time, Pallas kernels for 0%

profile of v1, /device:TPU:32, one launch (start us, length us, event | category | flops | bytes accessed | tf_op | source)
XLA Modules:
  0.0 997.2 jit_solution(3665384153753884899)
XLA Ops:
  8.1 24.5 %all_to_all.15 = bf16[32,64,256]{2,1,0:T(8,128)(2,1)S(1)} all-to-all(bf16[32,64,256]{2,1,0:T(8,128)(2,1)S(1)} %stack.6), channel_id=1, replica_groups=mesh['row'=32,'col'=16] {'row'}, dimensions={0} | all-to-all | bytes 2097152 | tf_op jit(solution)/shard_map/all_to_all | solution.py:12
  32.5 4.5 fusion.64
  37.1 70.3 %reduce-scatter.6.cloned.1.call-done = f32[64,256]{1,0:T(8,128)} async-done(((f32[1024,256]{1,0:T(8,128)}), f32[64,256]{1,0:T(8,128)}) %reduce-scatter.6.cloned.1.call-update) | async-done | bytes 65552 | tf_op jit(solution)/shard_map/reduce_scatter | solution.py:22
  108.4 24.2 %all_to_all.16 = bf16[32,64,256]{2,1,0:T(8,128)(2,1)S(1)} all-to-all(bf16[32,64,256]{2,1,0:T(8,128)(2,1)S(1)} %stack.7), channel_id=1, replica_groups=mesh['row'=32,'col'=16] {'row'}, dimensions={0} | all-to-all | bytes 2097152 | tf_op jit(solution)/shard_map/all_to_all | solution.py:12
  132.6 3.5 convolution_bitcast_fusion.1
  136.1 1.3 copy.15
  137.5 64.7 %reduce-scatter.10.cloned.1.call-done = f32[64,256]{1,0:T(8,128)} async-done(((f32[1024,256]{1,0:T(8,128)}), f32[64,256]{1,0:T(8,128)}) %reduce-scatter.10.cloned.1.call-update) | async-done | bytes 65552 | tf_op jit(solution)/shard_map/reduce_scatter | solution.py:22
  203.1 24.3 %all_to_all.17 = bf16[32,64,256]{2,1,0:T(8,128)(2,1)S(1)} all-to-all(bf16[32,64,256]{2,1,0:T(8,128)(2,1)S(1)} %stack.8), channel_id=1, replica_groups=mesh['row'=32,'col'=16] {'row'}, dimensions={0} | all-to-all | bytes 2097152 | tf_op jit(solution)/shard_map/all_to_all | solution.py:12
  227.4 5.0 convolution_bitcast_fusion
  233.1 64.1 %reduce-scatter.8.cloned.1.call-done = f32[64,256]{1,0:T(8,128)} async-done(((f32[1024,256]{1,0:T(8,128)}), f32[64,256]{1,0:T(8,128)}) %reduce-scatter.8.cloned.1.call-update) | async-done | bytes 65552 | tf_op jit(solution)/shard_map/reduce_scatter | solution.py:22
  297.2 1.5 multiply_subtract_fusion
  298.7 69.8 %all-gather.4.cloned.1.call-done = bf16[512,1024]{1,0:T(8,128)(2,1)} async-done(((bf16[32,1024]{1,0:T(8,128)(2,1)}), bf16[512,1024]{1,0:T(8,128)(2,1)}) %all-gather.4.cloned.1.call-update) | async-done | bytes 1048592 | tf_op jit(solution)/shard_map/all_gather | solution.py:34
  368.6 1.6 fusion.65
  370.2 69.0 %all-gather.6.cloned.1.call-done = f32[1024,256]{1,0:T(8,128)} async-done(((f32[64,256]{1,0:T(8,128)}), f32[1024,256]{1,0:T(8,128)}) %all-gather.6.cloned.1.call-update) | async-done | bytes 1048592 | tf_op jit(solution)/shard_map/all_gather | solution.py:35
  439.2 1.8 fusion.66
  441.8 127.1 %all-reduce.3.cloned.1.call-done = f32[768,32]{0,1:T(8,128)} async-done(((f32[768,32]{0,1:T(8,128)}), f32[768,32]{0,1:T(8,128)}) %all-reduce.3.cloned.1.call-update) | async-done | bytes 98320 | tf_op jit(solution)/shard_map/psum | solution.py:72
  568.9 1.0 iota_compare_fusion
  569.9 1.6 fusion.20
  571.5 1.1 fusion.24
  572.6 1.2 convolution_bitcast_fusion.2
  573.8 125.5 %psum.15 = f32[768,16]{0,1:T(8,128)S(1)} all-reduce(f32[768,16]{0,1:T(8,128)S(1)} %maximum_multiply_fusion.1), channel_id=1, replica_groups=mesh['row'=32,'col'=16] {'row'}, use_global_device_ids=true, to_apply=%region_4.0 | all-reduce | flops 12288 | bytes 98304 | tf_op jit(solution)/shard_map/psum | solution.py:72
  699.3 36.1 %all_gather.15 = f32[768,256]{0,1:T(8,128)} all-gather(f32[768,16]{0,1:T(8,128)S(1)} %psum.15), channel_id=1, replica_groups=mesh['row'=32,'col'=16] {'col'}, dimensions={1}, use_global_device_ids=true | all-gather | bytes 835584 | tf_op jit(solution)/shard_map/all_gather | solution.py:75
  735.4 1.6 constant_dynamic-update-slice_fusion.1
  737.1 2.1 copy.13
  739.2 2.0 fusion
  741.2 1.4 copy-done.4
  742.6 11.7 %cholesky.165 = f32[128,128]{1,0:T(8,128)S(1)} custom-call(f32[128,128]{1,0:T(8,128)S(1)} %cholesky.424), custom_call_target="Cholesky" | custom-call | tf_op jit(solution)/shard_map/jit(cholesky)/cholesky | solution.py:78
  754.4 9.8 custom-call.47
  764.3 1.4 constant_dynamic-update-slice_fusion.16
  765.7 1.4 convolution_subtract_fusion.4
  767.9 11.7 %cholesky.188 = f32[128,128]{1,0:T(8,128)S(1)} custom-call(f32[128,128]{1,0:T(8,128)S(1)} %cholesky.428), custom_call_target="Cholesky" | custom-call | tf_op jit(solution)/shard_map/jit(cholesky)/cholesky | solution.py:78
  779.6 10.0 %custom-call.48 = f32[1,128,128]{1,2,0:T(8,128)S(1)} custom-call(f32[1,128,128]{2,1,0:T(8,128)S(1)} %get-tuple-element.42), custom_call_target="InvertDiagBlocksLowerTriangular" | custom-call | tf_op jit(solution)/shard_map/jit(cholesky)/cholesky | solution.py:78
  789.6 1.3 convolution_dynamic-update-slice_fusion.1
  791.0 1.5 convolution_subtract_fusion.5
  793.2 11.7 %cholesky.354 = f32[128,128]{1,0:T(8,128)S(1)} custom-call(f32[128,128]{1,0:T(8,128)S(1)} %cholesky.433), custom_call_target="Cholesky" | custom-call | tf_op jit(solution)/shard_map/jit(cholesky)/cholesky | solution.py:78
  805.7 9.8 custom-call.49
  815.5 1.2 convolution_dynamic-update-slice_fusion.2
  816.7 1.6 convolution_subtract_fusion.6
  819.0 12.1 %cholesky.373 = f32[128,128]{1,0:T(8,128)S(1)} custom-call(f32[128,128]{1,0:T(8,128)S(1)} %cholesky.438), custom_call_target="Cholesky" | custom-call | tf_op jit(solution)/shard_map/jit(cholesky)/cholesky | solution.py:78
  831.8 9.8 custom-call.50
  841.6 1.2 convolution_dynamic-update-slice_fusion.3
  842.8 1.5 convolution_subtract_fusion.7
  844.9 13.2 %cholesky.392 = f32[128,128]{1,0:T(8,128)} custom-call(f32[128,128]{1,0:T(8,128)} %cholesky.443), custom_call_target="Cholesky" | custom-call | tf_op jit(solution)/shard_map/jit(cholesky)/cholesky | solution.py:78
  858.1 1.5 select_reduce_fusion.1
  860.2 11.3 %custom-call.51 = f32[1,128,128]{1,2,0:T(8,128)} custom-call(f32[1,128,128]{2,1,0:T(8,128)} %get-tuple-element.33), custom_call_target="InvertDiagBlocksLowerTriangular" | custom-call | tf_op jit(solution)/shard_map/jit(cholesky)/cholesky | solution.py:78
  871.5 1.0 convolution_dynamic-update-slice_fusion.4
  872.6 1.3 convolution_subtract_fusion.8
  873.9 11.9 %cholesky.410 = f32[128,128]{1,0:T(8,128)S(1)} custom-call(f32[128,128]{1,0:T(8,128)S(1)} %convolution_subtract_fusion.8), custom_call_target="Cholesky" | custom-call | tf_op jit(solution)/shard_map/jit(cholesky)/cholesky | solution.py:78
  891.1 1.6 select_select_fusion
  892.7 21.5 %while.1 = (s32[]{:T(128)}, f32[768,768]{1,0:T(8,128)}, s32[6,2]{0,1:T(2,128)S(1)}, f32[6,128,128]{2,1,0:T(8,128)}, s32[]{:T(128)}) while((s32[]{:T(128)}, f32[768,768]{1,0:T(8,128)}, s32[6,2]{0,1:T(2,128)S(1)}, f32[6,128,128]{2,1,0:T(8,128)}, s32[]{:T(128)}) %tuple.44), condition=%wide.while_cond, body=%wide.while_body.sunk | while | flops 2 | bytes 132705 | solution.py:80
  893.4 3.0 bitcast_dynamic-update-slice_fusion.2
  897.1 2.9 bitcast_dynamic-update-slice_fusion.2
  900.6 2.9 bitcast_dynamic-update-slice_fusion.2
  904.2 2.9 bitcast_dynamic-update-slice_fusion.2
  907.8 2.9 bitcast_dynamic-update-slice_fusion.2
  911.4 2.9 bitcast_dynamic-update-slice_fusion.2
  914.3 60.4 %custom-call.52 = f32[6,128,128]{1,2,0:T(8,128)} custom-call(f32[6,128,128]{2,1,0:T(8,128)} %get-tuple-element.9), custom_call_target="InvertDiagBlocksLowerTriangular" | custom-call | tf_op jit(solution)/shard_map/jit(_solve_triangular)/triangular_solve | solution.py:80
  974.7 1.3 constant_dynamic-update-slice_fusion.6
  976.0 1.5 convolution_subtract_fusion.2
  978.0 1.5 convolution_subtract_fusion.3
  980.1 1.8 convolution_subtract_fusion.1
  982.4 2.0 fusion.9
  984.9 2.3 convolution_subtract_fusion
  988.4 1.8 convolution_add_fusion
  (83 shorter events, 18.2 us)
Async XLA Ops:
  7.2 100.3 %reduce-scatter.6.cloned.1.call-start = ((), (), s32[]{:S(2)}) async-start(), calls=%async_computation.6 | async-start | bytes 1114112 | tf_op jit(solution)/shard_map/reduce_scatter | solution.py:22
  37.0 165.1 %reduce-scatter.10.cloned.1.call-start = ((), (), s32[]{:S(2)}) async-start(), calls=%async_computation.12 | async-start | bytes 1114112 | tf_op jit(solution)/shard_map/reduce_scatter | solution.py:22
  137.4 159.7 %reduce-scatter.8.cloned.1.call-start = ((), (), s32[]{:S(2)}) async-start(), calls=%async_computation.7 | async-start | bytes 1114112 | tf_op jit(solution)/shard_map/reduce_scatter | solution.py:22
  227.4 69.8 %copy-start.11 = (f32[64,256]{1,0:T(8,128)S(1)}, f32[64,256]{1,0:T(8,128)}, u32[]{:S(2)}) copy-start(f32[64,256]{1,0:T(8,128)} %reduce-scatter.6.cloned.1.call-done) | copy-start | bytes 196612
  227.4 141.2 %copy-start.9 = (bf16[32,1024]{1,0:T(8,128)(2,1)S(1)}, bf16[32,1024]{1,0:T(8,128)(2,1)}, u32[]{:S(2)}) copy-start(bf16[32,1024]{1,0:T(8,128)(2,1)} %param.5) | copy-start | bytes 196612
  232.4 136.1 %all-gather.4.cloned.1.call-start = ((), (), s32[]{:S(2)}) async-start(), calls=%async_computation.8 | async-start | bytes 1114112 | tf_op jit(solution)/shard_map/all_gather | solution.py:34
  233.0 206.2 %all-gather.6.cloned.1.call-start = ((), (), s32[]{:S(2)}) async-start(), calls=%async_computation.9 | async-start | bytes 1114112 | tf_op jit(solution)/shard_map/all_gather | solution.py:35
  298.7 270.2 %all-reduce.3.cloned.1.call-start = ((), (), s32[]{:S(2)}) async-start(), calls=%async_computation.10 | async-start | bytes 196608 | tf_op jit(solution)/shard_map/psum | solution.py:72
  439.2 132.3 %copy-start = (f32[1024,256]{1,0:T(8,128)S(1)}, f32[1024,256]{1,0:T(8,128)}, u32[]{:S(2)}) copy-start(f32[1024,256]{1,0:T(8,128)} %all-gather.6.cloned.1.call-done) | copy-start | bytes 3145732
  441.0 131.6 %copy-start.1 = (bf16[512,1024]{1,0:T(8,128)(2,1)S(1)}, bf16[512,1024]{1,0:T(8,128)(2,1)}, u32[]{:S(2)}) copy-start(bf16[512,1024]{1,0:T(8,128)(2,1)} %all-gather.4.cloned.1.call-done) | copy-start | bytes 3145732
  441.7 293.7 %all-gather.8.cloned.1.call-start = ((), (), s32[]{:S(2)}) async-start(), calls=%async_computation.11 | async-start | bytes 1671168 | tf_op jit(solution)/shard_map/all_gather | solution.py:74
  735.4 1.6 copy-start.5
  741.2 1.4 copy-start.4
  767.1 0.7 copy-start.6
  792.5 0.7 copy-start.7
  818.3 0.7 copy-start.8
  892.7 85.3 %copy-start.3 = (f32[768,768]{1,0:T(8,128)S(1)}, f32[768,768]{1,0:T(8,128)}, u32[]{:S(2)}) copy-start(f32[768,768]{1,0:T(8,128)} %fusion.20) | copy-start | bytes 7077892
  974.7 2.8 copy-start.10
  984.4 3.4 copy-start.2
Sparse Core Ops, SparseCore 0:
  37.2 70.2 reduce-scatter.5
  137.5 64.5 reduce-scatter.9
  232.6 64.5 reduce-scatter.7
  299.3 69.1 all-gather.3
  371.3 67.9 all-gather.5
  443.2 125.5 all-reduce.2
  570.9 71.5 all-gather.7
